TPU v7x, 128 devices: a whole 4x4x4 slice. The times are simulated.
128 devices in a mesh: img: 8 (over z, core), txt: 16 (over y, x).
Axes of the slice: x: 4, y: 4, z: 4, core: 2. Of those that a mesh axis runs over, the one named last changes fastest.
Arguments:
- image_emb: bfloat16 [196608, 1152], P(('img', 'txt')), may hold values from -0.1796875 to 0.1796875
- text_emb: bfloat16 [196608, 1152], P(('img', 'txt')), may hold values from -0.1796875 to 0.1796875
- row_weight: bfloat16 [196608], P(('img', 'txt')), may hold values from 0.5 to 6
- log_scale: float32 [1], replicated, may hold values from 1.6 to 2.4
- bias: float32 [1], replicated, may hold values from -4 to -2
- pair_slots: int32 [2048, 3], P(('img', 'txt')), may hold values from 0 to 3, as said below
Outputs:
- grad_image: bfloat16 [196608, 1152], P(('img', 'txt'))
- grad_text: bfloat16 [196608, 1152], P(('img', 'txt'))
- totals: float32 [3], replicated
Inputs may be any that keep to these rules, and one draw needn't show every extreme that they name: `pair_slots`: entries 0 and 1 are block numbers below 4; entry 2 is 0 or 1; a device's row at its own txt index has live 0; no device has more than 12 live rows, and in every draw some device has exactly 12.
All inputs are finite; a program needn't handle non-finite values.
Results may differ from a plain program's by a relative error of at most 0.009.
Values may be sent and summed in bfloat16 or wider, within the bound.
No kernel may reach another device: no remote copies, remote signals or barrier semaphores. Data moves between devices by JAX's collectives and lax.ppermute only.
A program may use at most 192 MiB of HBM per device.

v0:
```python
import jax
import jax.numpy as jnp
from jax import lax
from jax.sharding import PartitionSpec as P

ROWS = 384
BLK = 4


EPS = 1e-06


def normalize(emb):
    values = emb.astype(jnp.float32)
    inverse = lax.rsqrt(jnp.sum(values * values, axis=-1, keepdims=True) + EPS)
    return (values * inverse).astype(jnp.bfloat16)


def pair_tiles(image_blk, text_blk, weights, scale, offset, positive):
    sims = jnp.dot(image_blk, text_blk.T, preferred_element_type=jnp.float32)
    logits = scale * sims + offset
    eye = jnp.eye(image_blk.shape[0], dtype=jnp.float32)
    signs = 2.0 * positive * eye - 1.0
    wcol = weights[:, None]
    loss = -wcol * jax.nn.log_sigmoid(signs * logits)
    grads = -wcol * signs * jax.nn.sigmoid(-signs * logits)
    scaled = (scale * grads).astype(jnp.bfloat16)
    d_image = jnp.dot(scaled, text_blk, preferred_element_type=jnp.float32)
    d_text = jnp.dot(scaled.T, image_blk, preferred_element_type=jnp.float32)
    stats = jnp.stack([jnp.sum(loss), jnp.sum(grads * scale * sims), jnp.sum(grads)])
    return (d_image, d_text, stats)


def negative_pair(image_blk, text_blk, weights, live, scale, offset):

    def work(unused):
        d_image, d_text, stats = pair_tiles(image_blk, text_blk, weights, scale, offset, 0.0)
        return (d_image.astype(jnp.bfloat16), d_text.astype(jnp.bfloat16), stats)

    def skip(unused):
        empty = jnp.zeros(image_blk.shape, jnp.bfloat16)
        return (empty, empty, jnp.zeros((3,), jnp.float32))

    return lax.cond(live > 0, work, skip, 0)


def backprop_norm(emb, grad_hat):
    values = emb.astype(jnp.float32)
    inverse = lax.rsqrt(jnp.sum(values * values, axis=-1, keepdims=True) + EPS)
    unit = values * inverse
    inner = jnp.sum(unit * grad_hat, axis=-1, keepdims=True)
    return (inverse * (grad_hat - unit * inner)).astype(jnp.bfloat16)


def collect(tiles, targets, live):
    selector = (
        (targets[:, None] == jnp.arange(BLK, dtype=jnp.int32)[None, :]) & (live[:, None] > 0)
    ).astype(jnp.bfloat16)
    return jnp.einsum("sb,srd->brd", selector, tiles, preferred_element_type=jnp.float32)


def per_device(image_emb, text_emb, row_weight, log_scale, bias, pair_slots):
    width = image_emb.shape[1]
    scale = jnp.exp(log_scale[0])
    offset = bias[0]
    image_hat = normalize(image_emb).reshape(BLK, ROWS, width)
    text_hat = normalize(text_emb).reshape(BLK, ROWS, width)
    weights = row_weight.astype(jnp.float32).reshape(BLK, ROWS)
    image_tiles = []
    text_tiles = []
    stats = jnp.zeros((3,), jnp.float32)
    for block in range(BLK):
        d_image, d_text, part = pair_tiles(
            image_hat[block], text_hat[block], weights[block], scale, offset, 1.0
        )
        image_tiles.append(d_image)
        text_tiles.append(d_text)
        stats = stats + part
    image_acc = jnp.stack(image_tiles)
    text_acc = jnp.stack(text_tiles)
    asked = lax.all_to_all(pair_slots, "txt", split_axis=0, concat_axis=0, tiled=True)
    outgoing = jnp.take(text_hat, asked[:, 1], axis=0)
    fetched = lax.all_to_all(outgoing, "txt", split_axis=0, concat_axis=0, tiled=True)

    def visit(carry, item):
        acc, totals = carry
        text_blk, entry = item
        chosen = entry[0]
        d_image, d_text, part = negative_pair(
            image_hat[chosen], text_blk, weights[chosen], entry[2], scale, offset
        )
        acc = acc.at[chosen].add(d_image.astype(jnp.float32))
        return ((acc, totals + part), d_text)

    (image_acc, stats), text_out = lax.scan(visit, (image_acc, stats), (fetched, pair_slots))
    returned = lax.all_to_all(text_out, "txt", split_axis=0, concat_axis=0, tiled=True)
    text_acc = text_acc + collect(returned, asked[:, 1], asked[:, 2])
    summed = lax.psum(stats, ("img", "txt"))
    count = BLK * ROWS * lax.axis_size("img") * lax.axis_size("txt")
    grad_image = backprop_norm(image_emb, image_acc.reshape(BLK * ROWS, width))
    grad_text = backprop_norm(text_emb, text_acc.reshape(BLK * ROWS, width))
    return (grad_image, grad_text, summed / count)


def solution(mesh):
    return jax.shard_map(
        per_device,
        mesh=mesh,
        in_specs=(
            P(("img", "txt"), None),
            P(("img", "txt"), None),
            P(("img", "txt")),
            P(),
            P(),
            P(("img", "txt"), None),
        ),
        out_specs=(P(("img", "txt"), None), P(("img", "txt"), None), P()),
        check_vma=False,
    )
```

profile of v0, /device:TPU:1, one launch (start us, length us, event | category | flops | bytes accessed | tf_op | source)
XLA Modules:
  0.0 831.8 jit_solution(10530106217338440116)
XLA Ops:
  2.0 7.6 all-to-all-start
  19.0 7.0 gather_fusion
  26.0 13.2 %broadcast_select_fusion = bf16[16,384,1152]{2,1,0:T(8,128)(2,1)} fusion(bf16[16,384,1152]{2,1,0:T(8,128)(2,1)} %gather_fusion, pred[16]{0:T(512)(128)(4,1)S(1)} %get-tuple-element.183), kind=kLoop, calls=%fused_computation.37 | loop fusion | flops 7077888 | bytes 28311568 | tf_op jit(solution)/shard_map/jit(_take)/select_n | solution.py:82
  39.1 6.0 all-to-all-start.1
  61.7 8.1 fusion.77
  76.2 176.0 %all-to-all-done.1 = bf16[16,384,1152]{2,1,0:T(8,128)(2,1)} async-done(((bf16[16,384,1152]{2,1,0:T(8,128)(2,1)}), bf16[16,384,1152]{2,1,0:T(8,128)(2,1)}, u32[]{:S(2)}, u32[]{:S(2)}) %all-to-all-start.1) | async-done | bytes 14155808 | tf_op jit(solution)/shard_map/all_to_all | solution.py:83
  252.2 161.7 %while.15 = (s32[]{:T(128)}, f32[4,384,1152]{2,1,0:T(8,128)}, f32[3]{0:T(128)S(1)}, bf16[16,384,1152]{2,1,0:T(8,128)(2,1)}, s32[16,3]{0,1:T(4,128)S(1)}, /*index...) while((s32[]{:T(128)}, f32[4,384,1152]{2,1,0:T(8,128)}, ...), condition=%wide.region_21.22_spmd, body=%wide.region_14.21_spmd.sunk | while | flops 1026884352 | bytes 15059874 | solution.py:95
  256.6 3.5 fusion.87
  265.3 3.5 fusion.87
  273.9 3.5 fusion.87
  282.5 3.5 fusion.87
  290.2 11.7 %conditional.2 = (f32[3]{0:T(128)S(1)}, f32[1,384,1152]{2,1,0:T(8,128)S(1)}, bf16[1,384,1152]{2,1,0:T(8,128)(2,1)S(1)}) conditional(s32[]{:T(128)} %bitcast.82, () %tuple.67, (f32[4,384]{1,0:T(4,128)}, s32[]{:T(128)}, f32[]{:T(128)}, bf16[4,384,1152]{2,1,0:T(8,128)(2,1)}, bf16[16,384,1152]{2,1,0:T(8,128)(2,1)}, /*index=5*/s32[]{:T(128)}, ...), branch_computations={%region_16.16_spmd, %region_17.20_spmd} | conditional | flops 1025999616 | bytes 7980096 | solution.py:44
  290.9 3.9 multiply_reduce_fusion
  302.7 3.5 fusion.87
  311.3 3.5 fusion.87
  319.9 3.5 fusion.87
  327.6 11.7 %conditional.2 = (f32[3]{0:T(128)S(1)}, f32[1,384,1152]{2,1,0:T(8,128)S(1)}, bf16[1,384,1152]{2,1,0:T(8,128)(2,1)S(1)}) conditional(s32[]{:T(128)} %bitcast.82, () %tuple.67, (f32[4,384]{1,0:T(4,128)}, s32[]{:T(128)}, f32[]{:T(128)}, bf16[4,384,1152]{2,1,0:T(8,128)(2,1)}, bf16[16,384,1152]{2,1,0:T(8,128)(2,1)}, /*index=5*/s32[]{:T(128)}, ...), branch_computations={%region_16.16_spmd, %region_17.20_spmd} | conditional | flops 1025999616 | bytes 7980096 | solution.py:44
  328.3 3.9 multiply_reduce_fusion
  340.1 3.5 fusion.87
  348.7 3.5 fusion.87
  357.4 3.5 fusion.87
  366.1 3.5 fusion.87
  374.7 3.5 fusion.87
  383.4 3.5 fusion.87
  392.1 3.5 fusion.87
  400.8 3.5 fusion.87
  409.4 3.5 fusion.87
  414.4 118.8 %all-to-all-start.2 = ((bf16[16,384,1152]{2,1,0:T(8,128)(2,1)}), bf16[16,384,1152]{2,1,0:T(8,128)(2,1)}, u32[]{:S(2)}, u32[]{:S(2)}) async-start(bf16[16,384,1152]{2,1,0:T(8,128)(2,1)} %get-tuple-element.138), calls=%async_computation.2 | async-start | bytes 28311552 | tf_op jit(solution)/shard_map/all_to_all | solution.py:96
  545.0 252.3 %psum.7 = f32[3]{0:T(128)S(1)} all-reduce(f32[3]{0:T(128)} %copy-done.18), channel_id=1, replica_groups=mesh['img'=8,'txt'=16] {'img','txt'}, use_global_device_ids=true, to_apply=%region_24.25 | all-reduce | flops 3 | bytes 24 | tf_op jit(solution)/shard_map/psum | solution.py:98
  797.8 5.4 fusion.28
  806.6 16.3 %fusion.20 = f32[4,384,1152]{2,0,1:T(4,128)} fusion(bf16[16,384,1152]{2,1,0:T(8,128)(2,1)} %all-to-all-done.2, s32[16]{0:T(128)S(1)} %copy-done.16, pred[16]{0:T(512)(128)(4,1)S(1)} %copy-done.9), kind=kOutput, calls=%fused_computation.35 | convolution fusion | flops 56623232 | bytes 21233744 | tf_op jit(solution)/shard_map/sb,srd->brd/dot_general | solution.py:59
  823.0 5.0 maximum_add_fusion
  (235 shorter events, 112.0 us)
Async XLA Ops:
  2.0 13.9 %all-to-all-start = ((s32[16,1,3]{2,1,0:T(1,128)}), s32[16,1,3]{2,1,0:T(1,128)S(1)}, u32[]{:S(2)}, u32[]{:S(2)}) async-start(s32[16,1,3]{2,1,0:T(1,128)} %copy.11), calls=%async_computation | async-start | bytes 16384 | tf_op jit(solution)/shard_map/all_to_all | solution.py:81
  39.1 213.1 %all-to-all-start.1 = ((bf16[16,384,1152]{2,1,0:T(8,128)(2,1)}), bf16[16,384,1152]{2,1,0:T(8,128)(2,1)}, u32[]{:S(2)}, u32[]{:S(2)}) async-start(bf16[16,384,1152]{2,1,0:T(8,128)(2,1)} %broadcast_select_fusion), calls=%async_computation.1 | async-start | bytes 28311552 | tf_op jit(solution)/shard_map/all_to_all | solution.py:83
  48.4 21.3 %copy-start.12 = (f32[384]{0:T(512)}, f32[384]{0:T(512)S(1)}, u32[]{:S(2)}) copy-start(f32[384]{0:T(512)S(1)} %get-tuple-element.181) | copy-start | bytes 4612
  48.5 22.1 %copy-start.10 = (f32[384]{0:T(512)}, f32[384]{0:T(512)S(1)}, u32[]{:S(2)}) copy-start(f32[384]{0:T(512)S(1)} %get-tuple-element.178) | copy-start | bytes 4612
  48.5 22.9 %copy-start.14 = (f32[384]{0:T(512)}, f32[384]{0:T(512)S(1)}, u32[]{:S(2)}) copy-start(f32[384]{0:T(512)S(1)} %get-tuple-element.180) | copy-start | bytes 4612
  48.5 23.8 %copy-start.15 = (f32[384]{0:T(512)}, f32[384]{0:T(512)S(1)}, u32[]{:S(2)}) copy-start(f32[384]{0:T(512)S(1)} %get-tuple-element.179) | copy-start | bytes 4612
  53.9 5.9 copy-start.2
  55.9 14.7 %copy-start.19 = (f32[384,384]{1,0:T(8,128)}, f32[384,384]{1,0:T(8,128)S(1)}, u32[]{:S(2)}) copy-start(f32[384,384]{1,0:T(8,128)S(1)} %get-tuple-element.186) | copy-start | bytes 1769476
  57.8 12.0 %copy-start.21 = (f32[384,384]{1,0:T(8,128)}, f32[384,384]{1,0:T(8,128)S(1)}, u32[]{:S(2)}) copy-start(f32[384,384]{1,0:T(8,128)S(1)} %get-tuple-element.187) | copy-start | bytes 1769476
  59.8 11.7 %copy-start.23 = (f32[384,384]{1,0:T(8,128)}, f32[384,384]{1,0:T(8,128)S(1)}, u32[]{:S(2)}) copy-start(f32[384,384]{1,0:T(8,128)S(1)} %get-tuple-element.188) | copy-start | bytes 1769476
  61.7 10.5 %copy-start.24 = (f32[384,384]{1,0:T(8,128)}, f32[384,384]{1,0:T(8,128)S(1)}, u32[]{:S(2)}) copy-start(f32[384,384]{1,0:T(8,128)S(1)} %get-tuple-element.189) | copy-start | bytes 1769476
  73.1 179.2 %copy-start.7 = (s32[16,3]{0,1:T(4,128)S(1)}, s32[16,3]{0,1:T(4,128)}, u32[]{:S(2)}) copy-start(s32[16,3]{0,1:T(4,128)} %param.17) | copy-start | bytes 580
  73.1 179.1 %copy-start.8 = (s32[3]{0:T(128)S(1)}, s32[3]{0:T(128)}, u32[]{:S(2)}) copy-start(s32[3]{0:T(128)} %constant.96.clone.1) | copy-start | bytes 40
  73.1 179.1 %copy-start.17 = (f32[3]{0:T(128)S(1)}, f32[3]{0:T(128)}, u32[]{:S(2)}) copy-start(f32[3]{0:T(128)} %fusion.77) | copy-start | bytes 40
  413.9 0.5 copy-start.18
  414.4 118.8 %copy-start.3 = (bf16[4,384,1152]{2,1,0:T(8,128)(2,1)S(1)}, bf16[4,384,1152]{2,1,0:T(8,128)(2,1)}, u32[]{:S(2)}) copy-start(bf16[4,384,1152]{2,1,0:T(8,128)(2,1)} %get-tuple-element.319) | copy-start | bytes 10616836
  414.4 392.1 %all-to-all-start.2 = ((bf16[16,384,1152]{2,1,0:T(8,128)(2,1)}), bf16[16,384,1152]{2,1,0:T(8,128)(2,1)}, u32[]{:S(2)}, u32[]{:S(2)}) async-start(bf16[16,384,1152]{2,1,0:T(8,128)(2,1)} %get-tuple-element.138), calls=%async_computation.2 | async-start | bytes 28311552 | tf_op jit(solution)/shard_map/all_to_all | solution.py:96
  533.2 6.4 copy-start.13
  533.2 6.4 copy-start.22
  536.5 5.2 copy-start.11
  536.5 5.2 copy-start.20
  541.7 261.6 %slice-start = ((s8[7077888]{0:T(1024)(128)(4,1)}), s8[2883584]{0:T(1024)(128)(4,1)S(1)}, s32[]{:S(2)}) async-start(s8[7077888]{0:T(1024)(128)(4,1)} %bitcast.96), calls=%async_computation.3 | async-start | bytes 5767168
  797.3 5.9 copy-start
  797.8 6.0 slice-start.1
  803.8 2.8 copy-start.9
  803.8 2.8 copy-start.16
  806.6 16.4 %copy-start.4 = (f32[1,384,1152]{2,1,0:T(8,128)S(1)}, f32[1,384,1152]{2,1,0:T(8,128)}, u32[]{:S(2)}) copy-start(f32[1,384,1152]{2,1,0:T(8,128)} %convolution_bitcast_fusion) | copy-start | bytes 5308420
  806.6 16.4 %copy-start.5 = (f32[1,384,1152]{2,1,0:T(8,128)S(1)}, f32[1,384,1152]{2,1,0:T(8,128)}, u32[]{:S(2)}) copy-start(f32[1,384,1152]{2,1,0:T(8,128)} %convolution_bitcast_fusion.1) | copy-start | bytes 5308420
  806.6 16.3 %copy-start.6 = (f32[1,384,1152]{2,1,0:T(8,128)S(1)}, f32[1,384,1152]{2,1,0:T(8,128)}, u32[]{:S(2)}) copy-start(f32[1,384,1152]{2,1,0:T(8,128)} %convolution_bitcast_fusion.2) | copy-start | bytes 5308420
  823.0 5.0 copy-start.1
where the time goes:
time: 836 us; the launch traced here: 832 us
  blocking collectives  252 us (30%)
  waiting for transfers between devices  177 us (21%)
  starting transfers between devices  132 us (16%)
  other arithmetic  129 us (15%)
  matrix products  57.2 us (7%)
  loops' own time  41.2 us (5%)
  local copies, waits for them, and re-layouts  40.5 us (5%)
    psum x1, blocking collectives, per_device(): summed = lax.psum(stats, ('img', 'txt'))  252 us
    all_to_all x1, waiting for transfers between devices, per_device(): lax.all_to_all(outgoing, 'txt', split_axis=0, concat_axis=0, tiled=True)  176 us
    all_to_all x1, starting transfers between devices, per_device(): lax.all_to_all(text_out, 'txt', split_axis=0, concat_axis=0, tiled=True)  119 us
    scatter-add x16, other arithmetic, visit(): acc = acc.at[chosen].add(d_image.astype(jnp.float32))  56 us
    another operation x1, loops' own time, per_device(): lax.scan(visit, (image_acc, stats), (fetched, pair_slots))  40.6 us
    dot_general x6, matrix products, pair_tiles(): d_text = jnp.dot(scaled.T, image_blk, preferred_element_type=jnp.float32)  16.9 us
  transfers between devices with their start and end apart: 3, of which 2 were waited for; matrix products, arithmetic and copies ran while one was open for 7% of the time, Pallas kernels for 0%

commit v1 on v0

v1 whole, which is shorter than its diff:
```python
import functools

import jax
import jax.numpy as jnp
from jax import lax
from jax.experimental import pallas as pl
from jax.experimental.pallas import tpu as pltpu
from jax.sharding import PartitionSpec as P

ROWS = 384
BLK = 4
SIDE = 4
HALF = BLK // 2
EPS = 1e-06
VMEM = 60 * 1024 * 1024
CHUNK = 48

NEAR = (0, 1, 3)
FAR = 2
NEAR_SLOTS = tuple((i, j) for i in NEAR for j in NEAR if (i, j) != (0, 0))
FAR_X_SLOTS = tuple((FAR, j) for j in (0, 1, 3, 2))
FAR_Y_SLOTS = tuple((i, FAR) for i in NEAR)
ALL_SLOTS = NEAR_SLOTS + FAR_X_SLOTS + FAR_Y_SLOTS
SLOT_AT = {slot: at for at, slot in enumerate(ALL_SLOTS)}
N_SLOTS = len(ALL_SLOTS)
ANY = pl.BlockSpec(memory_space=pl.ANY)
SMEM = pl.BlockSpec(memory_space=pltpu.SMEM)
WHOLE = pl.BlockSpec(memory_space=pltpu.VMEM)


def params(flops, nbytes):
    return dict(
        compiler_params=pltpu.CompilerParams(vmem_limit_bytes=VMEM),
        cost_estimate=pl.CostEstimate(flops=flops, bytes_accessed=nbytes, transcendentals=0),
    )


def normalize_kernel(emb_ref, out_ref):
    values = emb_ref[...].astype(jnp.float32)
    inverse = lax.rsqrt(jnp.sum(values * values, axis=-1, keepdims=True) + EPS)
    out_ref[...] = (values * inverse).astype(jnp.bfloat16)


def normalize(emb):
    rows, width = emb.shape
    spec = pl.BlockSpec((ROWS, width), lambda g: (g, 0))
    return pl.pallas_call(
        normalize_kernel,
        grid=(rows // ROWS,),
        in_specs=[spec],
        out_specs=spec,
        out_shape=jax.ShapeDtypeStruct(emb.shape, jnp.bfloat16),
        **params(rows * width * 6, rows * width * 4),
    )(emb)


def block_copies(refs, offset, index, dst, sem):
    found = refs[offset]
    if len(found) == 1:
        rows = pl.ds(pl.multiple_of(index * ROWS, ROWS), ROWS)
        return [(None, pltpu.make_async_copy(found[0].at[rows], dst, sem))]
    copies = []
    for part in range(2):
        local = jnp.clip(index - part * HALF, 0, HALF - 1)
        rows = pl.ds(pl.multiple_of(local * ROWS, ROWS), ROWS)
        inside = (index >= part * HALF) & (index < (part + 1) * HALF)
        copies.append((inside, pltpu.make_async_copy(found[part].at[rows], dst, sem)))
    return copies


def start_copies(live, copies):
    for inside, copy in copies:
        go = live if inside is None else live & inside
        pl.when(go)(copy.start)


def split_refs(refs):
    return {0: refs[0:1], 1: refs[1:2], 2: refs[2:4], 3: refs[4:5]}


def coefficients(sims_ref, coef_ref, weight_ref, scale, offset, positive):
    def step(at, sums):
        loss_sum, coef_sum, dot_sum = sums
        rows = pl.ds(pl.multiple_of(at * CHUNK, CHUNK), CHUNK)
        sims = sims_ref[rows, :]
        logits = scale * sims + offset
        weight = jnp.concatenate([weight_ref[rows, :]] * (ROWS // 128), axis=1)
        scaled_weight = weight * scale
        if positive is not None:
            row = lax.broadcasted_iota(jnp.int32, sims.shape, 0) + at * CHUNK
            col = lax.broadcasted_iota(jnp.int32, sims.shape, 1)
            diagonal = (row == col) & (positive > 0)
            logits = jnp.where(diagonal, -logits, logits)
            scaled_weight = jnp.where(diagonal, -scaled_weight, scaled_weight)
        power = jnp.exp(logits)
        one_more = 1.0 + power
        coef = scaled_weight * (power / one_more)
        loss = weight * jnp.log(one_more)
        coef_ref[rows, :] = coef.astype(jnp.bfloat16)

        def fold(value):
            return jnp.sum(value.reshape(CHUNK // 8, 8, ROWS), axis=0)

        return (loss_sum + fold(loss), coef_sum + fold(coef), dot_sum + fold(coef * sims))

    zero = jnp.zeros((8, ROWS), jnp.float32)
    return lax.fori_loop(0, ROWS // CHUNK, step, (zero, zero, zero))


def dot(lhs, rhs, dims):
    return lax.dot_general(lhs, rhs, (dims, ((), ())), preferred_element_type=jnp.float32)


NT = ((1,), (1,))
NN = ((1,), (0,))
TN = ((0,), (0,))


def pairs_kernel(slots, n_positive, out_axis, n_extra, *refs):
    meta, scalars, weights = refs[0:3]
    xrefs, yrefs = split_refs(refs[3:8]), split_refs(refs[8:13])
    at = 13
    extra_coef = refs[at] if n_extra else None
    at += 1 if n_extra else 0
    coef_out, stats_out = refs[at], refs[at + 1]
    at += 2
    grads = refs[at:at + 2] if out_axis else ()
    at += len(grads)
    xbuf, ybuf, wbuf, sims, sems = refs[at:at + 5]
    acc = refs[at + 5] if out_axis else None
    total = len(slots) + n_positive
    scale, offset = scalars[0], scalars[1]

    def entry(s):
        if s < len(slots):
            base = SLOT_AT[slots[s]]
            return base, slots[s]
        return N_SLOTS + s - len(slots), (0, 0)

    for s in range(total):
        row, (i, j) = entry(s)
        live = meta[row, 2] > 0
        p, q = meta[row, 0], meta[row, 1]
        start_copies(live, block_copies(xrefs, i, p, xbuf.at[s], sems.at[0, s]))
        start_copies(live, block_copies(yrefs, j, q, ybuf.at[s], sems.at[1, s]))
        rows = pl.ds(pl.multiple_of((i * BLK + p) * ROWS, ROWS), ROWS)
        start_copies(live, [(None, pltpu.make_async_copy(weights.at[rows], wbuf.at[s], sems.at[2, s]))])
    extra = ()
    if n_extra:
        row = SLOT_AT[(FAR, FAR)]
        live_extra = meta[row, 2] > 0
        extra = [(xbuf.at[total], sems.at[0, total]), (ybuf.at[total, :, :ROWS], sems.at[1, total])]
        start_copies(live_extra, block_copies(xrefs, FAR, meta[row, 0], *extra[0]))
        coef_copy = pltpu.make_async_copy(extra_coef.at[FAR_X_SLOTS.index((FAR, FAR))], *extra[1])
        start_copies(live_extra, [(None, coef_copy)])

    stats_out[...] = jnp.zeros_like(stats_out)
    if out_axis:
        for b in range(BLK):
            acc[b] = jnp.zeros_like(acc[b])

    first = SLOT_AT[slots[0]]

    def work(s, unused):
        row = jnp.where(s < len(slots), first + s, N_SLOTS + s - len(slots))

        @pl.when(meta[row, 2] > 0)
        def _():
            pltpu.make_async_copy(xrefs[0][0].at[pl.ds(0, ROWS)], xbuf.at[s], sems.at[0, s]).wait()
            pltpu.make_async_copy(yrefs[0][0].at[pl.ds(0, ROWS)], ybuf.at[s], sems.at[1, s]).wait()
            pltpu.make_async_copy(weights.at[pl.ds(0, ROWS)], wbuf.at[s], sems.at[2, s]).wait()
            sims[...] = dot(xbuf[s], ybuf[s], NT)
            positive = meta[row, 3] if n_positive else None
            sums = coefficients(sims, coef_out.at[s], wbuf.at[s], scale, offset, positive)
            for k in range(3):
                stats_out[k] += sums[k]
            if out_axis == "x":
                acc[meta[row, 0]] += dot(coef_out[s], ybuf[s], NN)
            if out_axis == "y":
                acc[meta[row, 1]] += dot(coef_out[s], xbuf[s], TN)

        return unused

    lax.fori_loop(0, total, work, 0)
    if n_extra:
        @pl.when(live_extra)
        def _():
            pltpu.make_async_copy(xrefs[0][0].at[pl.ds(0, ROWS)], *extra[0]).wait()
            pltpu.make_async_copy(extra_coef.at[0], *extra[1]).wait()
            acc[meta[SLOT_AT[(FAR, FAR)], 1]] += dot(ybuf[total, :, :ROWS], xbuf[total], TN)
    for b in range(BLK if out_axis else 0):
        grads[b // HALF][pl.ds(b % HALF * ROWS, ROWS), :] = acc[b].astype(jnp.bfloat16)


def pairs(slots, n_positive, out_axis, extra_coef, meta, scalars, weights, images, texts):
    width = images[0].shape[1]
    total = len(slots) + n_positive
    n_extra = 0 if extra_coef is None else 1
    out_shape = [
        jax.ShapeDtypeStruct((total, ROWS, ROWS), jnp.bfloat16),
        jax.ShapeDtypeStruct((3, 8, ROWS), jnp.float32),
    ]
    if out_axis:
        out_shape += [jax.ShapeDtypeStruct((HALF * ROWS, width), jnp.bfloat16)] * 2
    held = total + n_extra
    scratch = [
        pltpu.VMEM((held, ROWS, width), jnp.bfloat16),
        pltpu.VMEM((held, ROWS, width), jnp.bfloat16),
        pltpu.VMEM((total, ROWS, 128), jnp.float32),
        pltpu.VMEM((ROWS, ROWS), jnp.float32),
        pltpu.SemaphoreType.DMA((3, held)),
    ]
    if out_axis:
        scratch.append(pltpu.VMEM((BLK, ROWS, width), jnp.float32))
    operands = [meta, scalars, weights, *images, *texts]
    specs = [SMEM, SMEM] + [ANY] * 11
    if n_extra:
        operands.append(extra_coef)
        specs.append(ANY)
    matmuls = total + (held if out_axis else 0)
    return pl.pallas_call(
        functools.partial(pairs_kernel, slots, n_positive, out_axis, n_extra),
        in_specs=specs,
        out_specs=[WHOLE] * len(out_shape),
        out_shape=out_shape,
        scratch_shapes=scratch,
        **params(matmuls * 2 * ROWS * ROWS * width * 2, total * 2 * ROWS * width * 2),
    )(*operands)


def grads_kernel(axis, groups, sources, *refs):
    meta = refs[0]
    other = split_refs(refs[1:6])
    coefs = refs[6:6 + sources]
    outs = refs[6 + sources:6 + sources + len(groups)]
    buf, cbuf, acc, sems = refs[6 + sources + len(groups):]
    mine, theirs = (0, 1) if axis == "x" else (1, 0)
    at = 0
    for group in groups:
        for row, source, index, neighbour in group:
            live = meta[row, 2] > 0
            start_copies(live, block_copies(other, neighbour, meta[row, theirs], buf.at[at], sems.at[0, at]))
            copy = pltpu.make_async_copy(coefs[source].at[index], cbuf.at[at], sems.at[1, at])
            start_copies(live, [(None, copy)])
            at += 1
    at = 0
    for group, out in zip(groups, outs):
        for b in range(BLK):
            acc[b] = jnp.zeros_like(acc[b])
        for row, source, index, neighbour in group:

            @pl.when(meta[row, 2] > 0)
            def _():
                pltpu.make_async_copy(other[0][0].at[pl.ds(0, ROWS)], buf.at[at], sems.at[0, at]).wait()
                pltpu.make_async_copy(coefs[source].at[index], cbuf.at[at], sems.at[1, at]).wait()
                acc[meta[row, mine]] += dot(cbuf[at], buf[at], NN if axis == "x" else TN)

            at += 1
        for b in range(BLK):
            out[pl.ds(b * ROWS, ROWS), :] = acc[b].astype(out.dtype)


def grads(axis, offsets, with_positive, dtype, meta, blocks, near, far_x, far_y):
    width = blocks[0].shape[1]
    groups = []
    for offset in offsets:
        group = []
        for neighbour in (0, 1, 3, 2):
            slot = (offset, neighbour) if axis == "x" else (neighbour, offset)
            if slot == (0, 0):
                continue
            for source, known in enumerate((NEAR_SLOTS, FAR_X_SLOTS, FAR_Y_SLOTS)):
                if slot in known:
                    group.append((SLOT_AT[slot], source, known.index(slot), neighbour))
        if with_positive:
            for b in range(BLK):
                group.append((N_SLOTS + b, 0, len(NEAR_SLOTS) + b, 0))
        groups.append(tuple(group))
    total = sum(len(group) for group in groups)
    return pl.pallas_call(
        functools.partial(grads_kernel, axis, tuple(groups), 3),
        in_specs=[SMEM] + [ANY] * 8,
        out_specs=[WHOLE] * len(groups),
        out_shape=[jax.ShapeDtypeStruct((BLK * ROWS, width), dtype)] * len(groups),
        scratch_shapes=[
            pltpu.VMEM((total, ROWS, width), jnp.bfloat16),
            pltpu.VMEM((total, ROWS, ROWS), jnp.bfloat16),
            pltpu.VMEM((BLK, ROWS, width), jnp.float32),
            pltpu.SemaphoreType.DMA((2, total)),
        ],
        **params(total * 2 * ROWS * ROWS * width * 2, total * 2 * ROWS * width * 2),
    )(meta, *blocks, near, far_x, far_y)


def finish_kernel(emb_ref, own_ref, left_ref, right_ref, out_ref):
    values = emb_ref[...].astype(jnp.float32)
    inverse = lax.rsqrt(jnp.sum(values * values, axis=-1, keepdims=True) + EPS)
    unit = values * inverse
    total = own_ref[...] + left_ref[...].astype(jnp.float32) + right_ref[...].astype(jnp.float32)
    inner = jnp.sum(unit * total, axis=-1, keepdims=True)
    out_ref[...] = (inverse * (total - unit * inner)).astype(jnp.bfloat16)


def finish(emb, own, left, right):
    rows, width = emb.shape
    step = 256
    spec = pl.BlockSpec((step, width), lambda g: (g, 0))
    return pl.pallas_call(
        finish_kernel,
        grid=(rows // step,),
        in_specs=[spec] * 4,
        out_specs=spec,
        out_shape=jax.ShapeDtypeStruct(emb.shape, jnp.bfloat16),
        **params(rows * width * 12, rows * width * 12),
    )(emb, own, left, right)


def shift(value, axis, by):
    pairs_of = []
    for y in range(SIDE):
        for x in range(SIDE):
            to = (y * SIDE + (x + by) % SIDE) if axis == "x" else ((y + by) % SIDE * SIDE + x)
            pairs_of.append((y * SIDE + x, to))
    return lax.ppermute(value, "txt", pairs_of)


def after(values, done):
    out = lax.optimization_barrier(tuple(values) + tuple(done))
    return out[:len(values)]


def per_device(image_emb, text_emb, row_weight, log_scale, bias, pair_slots):
    half = HALF * ROWS
    scale = jnp.exp(log_scale[0])
    scalars = jnp.stack([scale, bias[0]])
    xh, yh = normalize(image_emb), normalize(text_emb)
    x_prev, x_next = shift(xh, "x", 1), shift(xh, "x", -1)
    y_prev, y_next = shift(yh, "y", 1), shift(yh, "y", -1)

    small = jnp.concatenate([row_weight.astype(jnp.float32), pair_slots.astype(jnp.float32).reshape(-1)])
    everyone = lax.all_gather(small, "txt", axis=0, tiled=False)
    me = lax.axis_index("txt")
    my_y, my_x = me // SIDE, me % SIDE
    row_devices = jnp.stack([my_y * SIDE + (my_x + i) % SIDE for i in range(SIDE)])
    row_data = jnp.take(everyone, row_devices, axis=0)
    weights = row_data[:, :BLK * ROWS].reshape(SIDE * BLK * ROWS, 1)
    weights = jnp.broadcast_to(weights, (SIDE * BLK * ROWS, 128))
    plans = row_data[:, BLK * ROWS:].reshape(SIDE, SIDE, SIDE, 3)
    plans = lax.dynamic_index_in_dim(plans, my_x, axis=2, keepdims=False)
    plans = jnp.roll(plans, -my_y, axis=1)
    table = [plans[i, j] for i, j in ALL_SLOTS]
    negative = jnp.concatenate([jnp.stack(table), jnp.zeros((N_SLOTS, 1), jnp.float32)], axis=1)
    numbers = jnp.arange(BLK, dtype=jnp.float32)
    positive = jnp.stack([numbers, numbers, jnp.ones(BLK), jnp.ones(BLK)], axis=1)
    meta = jnp.concatenate([negative, positive]).astype(jnp.int32)

    x_prev, x_next, y_prev, y_next = after((x_prev, x_next, y_prev, y_next), ())
    x_far = (shift(x_prev[:half], "x", 1), shift(x_next[half:], "x", -1))
    y_far = (shift(y_prev[:half], "y", 1), shift(y_next[half:], "y", -1))
    near_images = (xh, x_next, xh, xh, x_prev)
    near_texts = (yh, y_next, yh, yh, y_prev)
    near, near_stats = pairs(NEAR_SLOTS, BLK, None, None, meta, scalars, weights, near_images, near_texts)

    images = (xh, x_next, *x_far, x_prev)
    texts = (yh, y_next, *y_far, y_prev)
    far_x, far_x_stats, dx_a, dx_b = pairs(FAR_X_SLOTS, 0, "x", None, meta, scalars, weights, images, texts)
    dx_from_prev, dx_from_next = shift(dx_a, "x", 1), shift(dx_b, "x", -1)
    far_y, far_y_stats, dy_a, dy_b = pairs(FAR_Y_SLOTS, 0, "y", far_x, meta, scalars, weights, images, texts)
    dy_from_prev, dy_from_next = shift(dy_a, "y", 1), shift(dy_b, "y", -1)
    dx_next, dx_prev = grads("x", (1, 3), False, jnp.bfloat16, meta, texts, near, far_x, far_y)
    dy_next, dy_prev = grads("y", (1, 3), False, jnp.bfloat16, meta, images, near, far_x, far_y)

    def join(ours, arrived, lower):
        summed = (ours[:half] if lower else ours[half:]).astype(jnp.float32) + arrived.astype(jnp.float32)
        summed = summed.astype(jnp.bfloat16)
        return jnp.concatenate([summed, ours[half:]] if lower else [ours[:half], summed])

    back_x = (shift(join(dx_next, dx_from_prev, True), "x", 1), shift(join(dx_prev, dx_from_next, False), "x", -1))
    back_y = (shift(join(dy_next, dy_from_prev, True), "y", 1), shift(join(dy_prev, dy_from_next, False), "y", -1))
    (dx_own,) = grads("x", (0,), True, jnp.float32, meta, texts, near, far_x, far_y)
    (dy_own,) = grads("y", (0,), True, jnp.float32, meta, images, near, far_x, far_y)

    sums = jnp.sum((near_stats + far_x_stats + far_y_stats).reshape(3, -1), axis=1)
    stats = jnp.stack([sums[0], sums[2], sums[1] / scale])
    summed = lax.psum(stats, ("img", "txt"))
    count = BLK * ROWS * lax.axis_size("img") * lax.axis_size("txt")
    grad_image = finish(image_emb, dx_own, *back_x)
    grad_text = finish(text_emb, dy_own, *back_y)
    return (grad_image, grad_text, summed / count)


def solution(mesh):
    return jax.shard_map(
        per_device,
        mesh=mesh,
        in_specs=(
            P(("img", "txt"), None),
            P(("img", "txt"), None),
            P(("img", "txt")),
            P(),
            P(),
            P(("img", "txt"), None),
        ),
        out_specs=(P(("img", "txt"), None), P(("img", "txt"), None), P()),
        check_vma=False,
    )
```

time: 836 us -> 469 us (0.56)
  blocking collectives: 252 us -> 135 us
  other arithmetic: 129 us -> 19 us
  Pallas kernels: 0 us -> 98.1 us
  starting transfers between devices: 132 us -> 34.9 us
  waiting for transfers between devices: 177 us -> 117 us
  matrix products: 57.2 us -> 0 us
  loops' own time: 41.2 us -> 0 us
  between operations: 2.29 us -> 17.6 us
    all_to_all x3 -> x0, waiting for transfers between devices: 177 us -> none  [the longest x1 176 us: per_device(): lax.all_to_all(outgoing, 'txt', split_axis=0, concat_axis=0, tiled=True)]
    all_to_all x3 -> x0, starting transfers between devices: 132 us -> none  [the longest x1 119 us: per_device(): lax.all_to_all(text_out, 'txt', split_axis=0, concat_axis=0, tiled=True)]
    psum x1, blocking collectives: 252 us -> 135 us  [per_device(): summed = lax.psum(stats, ('img', 'txt'))]
    pallas_call x0 -> x11, Pallas kernels: none -> 98.1 us  [the longest x4 36.5 us: grads(): pl.pallas_call(functools.partial(grads_kernel, axis, tuple(groups), 3), i...]
    unnamed x0 -> x2, waiting for transfers between devices: none -> 80.3 us
    dot_general x19 -> x0, matrix products: 57.2 us -> none  [the longest x6 16.9 us: pair_tiles(): d_text = jnp.dot(scaled.T, image_blk, preferred_element_type=jnp.float32)]
    scatter-add x16 -> x0, other arithmetic: 56 us -> none  [visit(): acc = acc.at[chosen].add(d_image.astype(jnp.float32))]
    another operation x17 -> x0, loops' own time: 41.2 us -> none  [the longest x1 40.6 us: per_device(): lax.scan(visit, (image_acc, stats), (fetched, pair_slots))]
  transfers between devices with their start and end apart: 3 -> 17, of which waited for: 2 -> 8; matrix products, arithmetic and copies ran while one was open for 7% -> 11% of each run, Pallas kernels for 0% -> 14%
where the time goes in v1:
time: 469 us; the launch traced here: 462 us
  blocking collectives  135 us (29%)
  waiting for transfers between devices  117 us (25%)
  Pallas kernels  98.1 us (21%)
  local copies, waits for them, and re-layouts  41.1 us (9%)
  starting transfers between devices  34.9 us (7%)
  other arithmetic  19 us (4%)
  between operations  17.6 us (4%)
    psum x1, blocking collectives, per_device(): summed = lax.psum(stats, ('img', 'txt'))  135 us
    unnamed x2, waiting for transfers between devices  80.3 us
    pallas_call x4, Pallas kernels, grads(): pl.pallas_call(functools.partial(grads_kernel, axis, tuple(groups), 3), i...  36.5 us
    ppermute x16, waiting for transfers between devices, shift(): return lax.ppermute(value, 'txt', pairs_of)  36.2 us
    ppermute x16, starting transfers between devices, shift(): return lax.ppermute(value, 'txt', pairs_of)  34.9 us
    pallas_call x3, Pallas kernels, pairs(): pl.pallas_call(functools.partial(pairs_kernel, slots, n_positive, out_axi...  32.5 us
    pallas_call x2, Pallas kernels, finish(): pl.pallas_call(finish_kernel, grid=(rows // step,), in_specs=[spec] * 4,...  19.5 us
    unnamed x40, local copies, waits for them, and re-layouts  13.1 us
  transfers between devices with their start and end apart: 17, of which 8 were waited for; matrix products, arithmetic and copies ran while one was open for 11% of the time, Pallas kernels for 14%

profile of v1, /device:TPU:1, one launch (start us, length us, event | category | flops | bytes accessed | tf_op | source)
XLA Modules:
  0.0 462.2 jit_solution(11433697356522572481)
XLA Ops:
  7.2 4.8 %shard_map.86.refs_3_.refs_5_.refs_6_.refs_1_ = bf16[1536,1152]{1,0:T(8,128)(2,1)} custom-call(bf16[1536,1152]{1,0:T(8,128)(2,1)} %emb_ref.6), custom_call_target="tpu_custom_call" | custom-call | flops 10616832 | bytes 7077888 | tf_op jit(solution)/shard_map/pallas_call | solution.py:47
  12.0 2.0 collective-permute-start
  15.4 4.8 %shard_map.85.refs_8_.refs_10_.refs_11_.refs_1_ = bf16[1536,1152]{1,0:T(8,128)(2,1)} custom-call(bf16[1536,1152]{1,0:T(8,128)(2,1)} %emb_ref.7), custom_call_target="tpu_custom_call" | custom-call | flops 10616832 | bytes 7077888 | tf_op jit(solution)/shard_map/pallas_call | solution.py:47
  29.4 80.3 %all-reduce.4.cloned.1.call-done = f32[25344]{0:T(1024)} async-done(((f32[25344]{0:T(1024)}), f32[25344]{0:T(1024)}) %all-reduce.4.cloned.1.call-update) | async-done | bytes 101392
  111.4 2.1 gather_fusion
  116.6 4.1 slice.112
  121.0 2.8 slice.113
  123.8 2.4 collective-permute-start.5
  127.6 2.8 slice.116
  130.4 2.7 collective-permute-start.7
  146.9 13.0 %collective-permute-done.4.refs_10_.refs_3_ = bf16[768,1152]{1,0:T(8,128)(2,1)} collective-permute-done((bf16[768,1152]{1,0:T(8,128)(2,1)}, bf16[768,1152]{1,0:T(8,128)(2,1)}, u32[]{:S(2)}, u32[]{:S(2)}) %collective-permute-start.4) | collective-permute-done | bytes 1769504 | tf_op jit(solution)/shard_map/ppermute | solution.py:324
  161.7 4.3 collective-permute-done.6.refs_5_.refs_3_
  168.0 2.8 broadcast_in_dim.20.refs_2_
  170.8 10.0 %shard_map.88 = (bf16[4,384,384]{2,1,0:T(8,128)(2,1)}, f32[3,8,384]{2,1,0:T(8,128)}, bf16[768,1152]{1,0:T(8,128)(2,1)}, bf16[768,1152]{1,0:T(8,128)(2,1)}) custom-call(s32[19,4]{1,0:T(8,128)} %convert_element_type.47.refs_0_, f32[2]{0:T(128)} %pad_maximum_fusion.4.refs_1_, f32[6144,128]{1,0:T(8,128)} %broadcast_in_dim.20.refs_2_, ...), custom_call_target="tpu_custom_call" | custom-call | flops 5435817984 | bytes 7077888 | tf_op jit(solution)/shard_map/pallas_call | solution.py:221
  180.8 8.2 %shard_map.89 = (bf16[3,384,384]{2,1,0:T(8,128)(2,1)}, f32[3,8,384]{2,1,0:T(8,128)}, bf16[768,1152]{1,0:T(8,128)(2,1)}, bf16[768,1152]{1,0:T(8,128)(2,1)}) custom-call(s32[19,4]{1,0:T(8,128)} %convert_element_type.47.refs_0_, f32[2]{0:T(128)} %pad_maximum_fusion.4.refs_1_, f32[6144,128]{1,0:T(8,128)} %broadcast_in_dim.20.refs_2_, ...), custom_call_target="tpu_custom_call" | custom-call | flops 4756340736 | bytes 5308416 | tf_op jit(solution)/shard_map/pallas_call | solution.py:221
  189.0 2.9 collective-permute-start.14
  191.9 14.2 %shard_map.87 = (bf16[12,384,384]{2,1,0:T(8,128)(2,1)}, f32[3,8,384]{2,1,0:T(8,128)}) custom-call(s32[19,4]{1,0:T(8,128)} %convert_element_type.47.refs_0_, f32[2]{0:T(128)} %pad_maximum_fusion.4.refs_1_, f32[6144,128]{1,0:T(8,128)} %broadcast_in_dim.20.refs_2_, bf16[1536,1152]{1,0:T(8,128)(2,1)} %shard_map.86.refs_3_.refs_5_.refs_6_.refs_1_, ...), custom_call_target="tpu_custom_call" | custom-call | flops 8153726976 | bytes 21233664 | tf_op jit(solution)/shard_map/pallas_call | solution.py:221
  206.2 9.3 %shard_map.94 = (bf16[1536,1152]{1,0:T(8,128)(2,1)}, bf16[1536,1152]{1,0:T(8,128)(2,1)}) custom-call(s32[19,4]{1,0:T(8,128)} %convert_element_type.47.refs_0_, bf16[1536,1152]{1,0:T(8,128)(2,1)} %shard_map.86.refs_3_.refs_5_.refs_6_.refs_1_, bf16[1536,1152]{1,0:T(8,128)(2,1)} %collective-permute-done.1.refs_4_.refs_2_, bf16[768,1152]{1,0:T(8,128)(2,1)} %copy-done.1, ...), custom_call_target="tpu_custom_call" | custom-call | flops 5435817984 | bytes 14155776 | tf_op jit(solution)/shard_map/pallas_call | solution.py:280
  218.1 7.8 %collective-permute-start.10 = (bf16[768,1152]{1,0:T(8,128)(2,1)}, bf16[768,1152]{1,0:T(8,128)(2,1)}, u32[]{:S(2)}, u32[]{:S(2)}) collective-permute-start(bf16[768,1152]{1,0:T(8,128)(2,1)} %get-tuple-element.31), channel_id=1, source_target_pairs={{0,3},{1,0},{2,1},{3,2},{4,7},{5,4},{6,5},{7,6},{8,11},{9,8},{10,9... | collective-permute-start | bytes 5308424 | tf_op jit(solution)/shard_map/ppermute | solution.py:324
  225.9 7.3 %shard_map.91 = (bf16[1536,1152]{1,0:T(8,128)(2,1)}, bf16[1536,1152]{1,0:T(8,128)(2,1)}) custom-call(s32[19,4]{1,0:T(8,128)} %convert_element_type.47.refs_0_, bf16[1536,1152]{1,0:T(8,128)(2,1)} %shard_map.85.refs_8_.refs_10_.refs_11_.refs_1_, bf16[1536,1152]{1,0:T(8,128)(2,1)} %collective-permute-done.3.refs_9_.refs_2_, ...), custom_call_target="tpu_custom_call" | custom-call | flops 5435817984 | bytes 14155776 | tf_op jit(solution)/shard_map/pallas_call | solution.py:280
  238.8 2.1 pad_maximum_fusion.3
  240.8 4.6 collective-permute-start.15
  245.5 8.0 %collective-permute-done.12 = bf16[768,1152]{1,0:T(8,128)(2,1)} collective-permute-done((bf16[768,1152]{1,0:T(8,128)(2,1)}, bf16[768,1152]{1,0:T(8,128)(2,1)}, u32[]{:S(2)}, u32[]{:S(2)}) %collective-permute-start.12) | collective-permute-done | bytes 1769504 | tf_op jit(solution)/shard_map/ppermute | solution.py:324
  255.4 2.1 pad_maximum_fusion.2
  257.5 7.0 %collective-permute-done.10 = bf16[768,1152]{1,0:T(8,128)(2,1)} collective-permute-done((bf16[768,1152]{1,0:T(8,128)(2,1)}, bf16[768,1152]{1,0:T(8,128)(2,1)}, u32[]{:S(2)}, u32[]{:S(2)}) %collective-permute-start.10) | collective-permute-done | bytes 1769504 | tf_op jit(solution)/shard_map/ppermute | solution.py:324
  266.7 7.8 %collective-permute-start.11 = (bf16[1536,1152]{1,0:T(8,128)(2,1)S(1)}, bf16[1536,1152]{1,0:T(8,128)(2,1)}, u32[]{:S(2)}, u32[]{:S(2)}) collective-permute-start(bf16[1536,1152]{1,0:T(8,128)(2,1)S(1)} %pad_maximum_fusion.1), channel_id=1, source_target_pairs={{0,3},{1,0},{2,1},{3,2},{4,7},{5,4},{6,5},{7,6},{8,11},{9,8},{10,9... | collective-permute-start | bytes 10616840 | tf_op jit(solution)/shard_map/ppermute | solution.py:324
  275.1 2.0 pad_maximum_fusion
  279.9 134.9 %psum.7 = f32[3]{0:T(128)S(1)} all-reduce(f32[3]{0:T(128)S(1)} %pad_maximum_fusion.5), channel_id=1, replica_groups=mesh['img'=8,'txt'=16] {'img','txt'}, use_global_device_ids=true, to_apply=%region_1.2 | all-reduce | flops 3 | bytes 24 | tf_op jit(solution)/shard_map/psum | solution.py:385
  415.3 9.9 %shard_map.93.own_ref = f32[1536,1152]{1,0:T(8,128)} custom-call(s32[19,4]{1,0:T(8,128)} %convert_element_type.47.refs_0_, bf16[1536,1152]{1,0:T(8,128)(2,1)} %shard_map.86.refs_3_.refs_5_.refs_6_.refs_1_, bf16[1536,1152]{1,0:T(8,128)(2,1)} %collective-permute-done.1.refs_4_.refs_2_, bf16[768,1152]{1,0:T(8,128)(2,1)} %copy-done.1, ...), custom_call_target="tpu_custom_call" | custom-call | flops 4756340736 | bytes 12386304 | tf_op jit(solution)/shard_map/pallas_call | solution.py:280
  425.2 10.1 %shard_map.90.own_ref = f32[1536,1152]{1,0:T(8,128)} custom-call(s32[19,4]{1,0:T(8,128)} %convert_element_type.47.refs_0_, bf16[1536,1152]{1,0:T(8,128)(2,1)} %shard_map.85.refs_8_.refs_10_.refs_11_.refs_1_, bf16[1536,1152]{1,0:T(8,128)(2,1)} %collective-permute-done.3.refs_9_.refs_2_, bf16[768,1152]{1,0:T(8,128)(2,1)} %collective-permute-done.4.refs_10_.refs_3_, ...), custom_call_target="tpu_custom_call" | custom-call | flops 4756340736 | bytes 12386304 | tf_op jit(solution)/shard_map/pallas_call | solution.py:280
  435.4 9.8 %shard_map.95 = bf16[1536,1152]{1,0:T(8,128)(2,1)} custom-call(bf16[1536,1152]{1,0:T(8,128)(2,1)} %emb_ref.7, f32[1536,1152]{1,0:T(8,128)} %shard_map.93.own_ref, bf16[1536,1152]{1,0:T(8,128)(2,1)} %collective-permute-done.13.left_ref, bf16[1536,1152]{1,0:T(8,128)(2,1)} %collective-permute-done.15.right_ref), custom_call_target="tpu_custom_call" | custom-call | flops 21233664 | bytes 21233664 | tf_op jit(solution)/shard_map/pallas_call | solution.py:308
  445.2 9.8 %shard_map.92 = bf16[1536,1152]{1,0:T(8,128)(2,1)} custom-call(bf16[1536,1152]{1,0:T(8,128)(2,1)} %emb_ref.6, f32[1536,1152]{1,0:T(8,128)} %shard_map.90.own_ref, bf16[1536,1152]{1,0:T(8,128)(2,1)} %collective-permute-done.9.left_ref, bf16[1536,1152]{1,0:T(8,128)(2,1)} %collective-permute-done.11.right_ref), custom_call_target="tpu_custom_call" | custom-call | flops 21233664 | bytes 21233664 | tf_op jit(solution)/shard_map/pallas_call | solution.py:308
  (102 shorter events, 48.0 us)
Async XLA Ops:
  7.2 102.6 %all-reduce.4.cloned.1.call-start = ((), (), s32[]{:S(2)}) async-start(), calls=%async_computation | async-start | bytes 204800
  12.0 11.0 %copy-start.14 = (s32[16,3]{0,1:T(4,128)S(1)}, s32[16,3]{0,1:T(4,128)}, u32[]{:S(2)}) copy-start(s32[16,3]{0,1:T(4,128)} %param.11) | copy-start | bytes 580
  12.0 11.2 %copy-start.13 = (bf16[1536]{0:T(1024)(128)(2,1)S(1)}, bf16[1536]{0:T(1024)(128)(2,1)}, u32[]{:S(2)}) copy-start(bf16[1536]{0:T(1024)(128)(2,1)} %param.8) | copy-start | bytes 9220
  12.0 104.6 %collective-permute-start = (bf16[1536,1152]{1,0:T(8,128)(2,1)}, bf16[1536,1152]{1,0:T(8,128)(2,1)S(1)}, u32[]{:S(2)}, u32[]{:S(2)}) collective-permute-start(bf16[1536,1152]{1,0:T(8,128)(2,1)} %shard_map.86.refs_3_.refs_5_.refs_6_.refs_1_), channel_id=1, source_target_pairs={{0,1},{1,2},{2,3},{3,0},{4,5},{5,6},{6,7},{7,4},{8,9},{9,10},{10,1... | collective-permute-start | bytes 10616840 | tf_op jit(solution)/shard_map/ppermute | solution.py:324
  14.0 102.5 %collective-permute-start.1 = (bf16[1536,1152]{1,0:T(8,128)(2,1)}, bf16[1536,1152]{1,0:T(8,128)(2,1)}, u32[]{:S(2)}, u32[]{:S(2)}) collective-permute-start(bf16[1536,1152]{1,0:T(8,128)(2,1)} %shard_map.86.refs_3_.refs_5_.refs_6_.refs_1_), channel_id=1, source_target_pairs={{0,3},{1,0},{2,1},{3,2},{4,7},{5,4},{6,5},{7,6},{8,11},{9,8},{10,9... | collective-permute-start | bytes 10616840 | tf_op jit(solution)/shard_map/ppermute | solution.py:324
  20.2 96.4 %collective-permute-start.2 = (bf16[1536,1152]{1,0:T(8,128)(2,1)}, bf16[1536,1152]{1,0:T(8,128)(2,1)}, u32[]{:S(2)}, u32[]{:S(2)}) collective-permute-start(bf16[1536,1152]{1,0:T(8,128)(2,1)} %shard_map.85.refs_8_.refs_10_.refs_11_.refs_1_), channel_id=1, source_target_pairs={{0,4},{1,5},{2,6},{3,7},{4,8},{5,9},{6,10},{7,11},{8,12},{9,13},{1... | collective-permute-start | bytes 10616840 | tf_op jit(solution)/shard_map/ppermute | solution.py:324
  21.6 95.0 %collective-permute-start.3 = (bf16[1536,1152]{1,0:T(8,128)(2,1)}, bf16[1536,1152]{1,0:T(8,128)(2,1)}, u32[]{:S(2)}, u32[]{:S(2)}) collective-permute-start(bf16[1536,1152]{1,0:T(8,128)(2,1)} %shard_map.85.refs_8_.refs_10_.refs_11_.refs_1_), channel_id=1, source_target_pairs={{0,12},{1,13},{2,14},{3,15},{4,0},{5,1},{6,2},{7,3},{8,4},{9,5},{1... | collective-permute-start | bytes 10616840 | tf_op jit(solution)/shard_map/ppermute | solution.py:324
  114.3 0.6 copy-start.8
  116.6 9.6 %copy-start = (bf16[1536,1152]{1,0:T(8,128)(2,1)}, bf16[1536,1152]{1,0:T(8,128)(2,1)S(1)}, u32[]{:S(2)}) copy-start(bf16[1536,1152]{1,0:T(8,128)(2,1)S(1)} %collective-permute-done.refs_7_.refs_5_) | copy-start | bytes 10616836
  120.7 39.1 %collective-permute-start.4 = (bf16[768,1152]{1,0:T(8,128)(2,1)}, bf16[768,1152]{1,0:T(8,128)(2,1)}, u32[]{:S(2)}, u32[]{:S(2)}) collective-permute-start(bf16[768,1152]{1,0:T(8,128)(2,1)} %slice.112), channel_id=1, source_target_pairs={{0,4},{1,5},{2,6},{3,7},{4,8},{5,9},{6,10},{7,11},{8,12},{9,13},{1... | collective-permute-start | bytes 5308424 | tf_op jit(solution)/shard_map/ppermute | solution.py:324
  123.8 10.0 %copy-start.9 = (f32[4,1584]{1,0:T(4,128)S(1)}, f32[4,1584]{1,0:T(4,128)}, u32[]{:S(2)}) copy-start(f32[4,1584]{1,0:T(4,128)} %copy-done.8) | copy-start | bytes 76036
  123.8 37.9 %collective-permute-start.5 = (bf16[768,1152]{1,0:T(8,128)(2,1)}, bf16[768,1152]{1,0:T(8,128)(2,1)}, u32[]{:S(2)}, u32[]{:S(2)}) collective-permute-start(bf16[768,1152]{1,0:T(8,128)(2,1)} %slice.113), channel_id=1, source_target_pairs={{0,12},{1,13},{2,14},{3,15},{4,0},{5,1},{6,2},{7,3},{8,4},{9,5},{1... | collective-permute-start | bytes 5308424 | tf_op jit(solution)/shard_map/ppermute | solution.py:324
  127.6 38.5 %collective-permute-start.6 = (bf16[768,1152]{1,0:T(8,128)(2,1)}, bf16[768,1152]{1,0:T(8,128)(2,1)S(1)}, u32[]{:S(2)}, u32[]{:S(2)}) collective-permute-start(bf16[768,1152]{1,0:T(8,128)(2,1)} %slice.115), channel_id=1, source_target_pairs={{0,1},{1,2},{2,3},{3,0},{4,5},{5,6},{6,7},{7,4},{8,9},{9,10},{10,1... | collective-permute-start | bytes 5308424 | tf_op jit(solution)/shard_map/ppermute | solution.py:324
  130.4 37.5 %collective-permute-start.7 = (bf16[768,1152]{1,0:T(8,128)(2,1)}, bf16[768,1152]{1,0:T(8,128)(2,1)S(1)}, u32[]{:S(2)}, u32[]{:S(2)}) collective-permute-start(bf16[768,1152]{1,0:T(8,128)(2,1)} %slice.116), channel_id=1, source_target_pairs={{0,3},{1,0},{2,1},{3,2},{4,7},{5,4},{6,5},{7,6},{8,11},{9,8},{10,9... | collective-permute-start | bytes 5308424 | tf_op jit(solution)/shard_map/ppermute | solution.py:324
  166.0 4.7 %copy-start.1 = (bf16[768,1152]{1,0:T(8,128)(2,1)}, bf16[768,1152]{1,0:T(8,128)(2,1)S(1)}, u32[]{:S(2)}) copy-start(bf16[768,1152]{1,0:T(8,128)(2,1)S(1)} %collective-permute-done.6.refs_5_.refs_3_) | copy-start | bytes 5308420
  168.0 2.8 copy-start.2
  189.0 46.8 %collective-permute-start.14 = (bf16[768,1152]{1,0:T(8,128)(2,1)}, bf16[768,1152]{1,0:T(8,128)(2,1)}, u32[]{:S(2)}, u32[]{:S(2)}) collective-permute-start(bf16[768,1152]{1,0:T(8,128)(2,1)} %get-tuple-element.35), channel_id=1, source_target_pairs={{0,12},{1,13},{2,14},{3,15},{4,0},{5,1},{6,2},{7,3},{8,4},{9,5},{1... | collective-permute-start | bytes 5308424 | tf_op jit(solution)/shard_map/ppermute | solution.py:324
  215.4 2.5 copy-start.5
  217.2 36.3 %collective-permute-start.12 = (bf16[768,1152]{1,0:T(8,128)(2,1)}, bf16[768,1152]{1,0:T(8,128)(2,1)}, u32[]{:S(2)}, u32[]{:S(2)}) collective-permute-start(bf16[768,1152]{1,0:T(8,128)(2,1)} %get-tuple-element.33), channel_id=1, source_target_pairs={{0,4},{1,5},{2,6},{3,7},{4,8},{5,9},{6,10},{7,11},{8,12},{9,13},{1... | collective-permute-start | bytes 5308424 | tf_op jit(solution)/shard_map/ppermute | solution.py:324
  218.1 46.4 %collective-permute-start.10 = (bf16[768,1152]{1,0:T(8,128)(2,1)}, bf16[768,1152]{1,0:T(8,128)(2,1)}, u32[]{:S(2)}, u32[]{:S(2)}) collective-permute-start(bf16[768,1152]{1,0:T(8,128)(2,1)} %get-tuple-element.31), channel_id=1, source_target_pairs={{0,3},{1,0},{2,1},{3,2},{4,7},{5,4},{6,5},{7,6},{8,11},{9,8},{10,9... | collective-permute-start | bytes 5308424 | tf_op jit(solution)/shard_map/ppermute | solution.py:324
  233.2 2.5 copy-start.3
  233.2 3.6 copy-start.7
  235.0 39.6 %collective-permute-start.8 = (bf16[768,1152]{1,0:T(8,128)(2,1)}, bf16[768,1152]{1,0:T(8,128)(2,1)S(1)}, u32[]{:S(2)}, u32[]{:S(2)}) collective-permute-start(bf16[768,1152]{1,0:T(8,128)(2,1)} %get-tuple-element.29), channel_id=1, source_target_pairs={{0,1},{1,2},{2,3},{3,0},{4,5},{5,6},{6,7},{7,4},{8,9},{9,10},{10,1... | collective-permute-start | bytes 5308424 | tf_op jit(solution)/shard_map/ppermute | solution.py:324
  238.8 14.7 %copy-start.6 = (bf16[1536,1152]{1,0:T(8,128)(2,1)S(1)}, bf16[1536,1152]{1,0:T(8,128)(2,1)}, u32[]{:S(2)}) copy-start(bf16[1536,1152]{1,0:T(8,128)(2,1)} %get-tuple-element.32) | copy-start | bytes 10616836
  240.8 194.5 %collective-permute-start.15 = (bf16[1536,1152]{1,0:T(8,128)(2,1)}, bf16[1536,1152]{1,0:T(8,128)(2,1)}, u32[]{:S(2)}, u32[]{:S(2)}) collective-permute-start(bf16[1536,1152]{1,0:T(8,128)(2,1)} %pad_maximum_fusion.3), channel_id=1, source_target_pairs={{0,12},{1,13},{2,14},{3,15},{4,0},{5,1},{6,2},{7,3},{8,4},{9,5},{1... | collective-permute-start | bytes 10616840 | tf_op jit(solution)/shard_map/ppermute | solution.py:324
  255.4 9.1 %copy-start.4 = (bf16[1536,1152]{1,0:T(8,128)(2,1)S(1)}, bf16[1536,1152]{1,0:T(8,128)(2,1)}, u32[]{:S(2)}) copy-start(bf16[1536,1152]{1,0:T(8,128)(2,1)} %get-tuple-element.30) | copy-start | bytes 10616836
  257.5 177.9 %collective-permute-start.13 = (bf16[1536,1152]{1,0:T(8,128)(2,1)}, bf16[1536,1152]{1,0:T(8,128)(2,1)}, u32[]{:S(2)}, u32[]{:S(2)}) collective-permute-start(bf16[1536,1152]{1,0:T(8,128)(2,1)} %pad_maximum_fusion.2), channel_id=1, source_target_pairs={{0,4},{1,5},{2,6},{3,7},{4,8},{5,9},{6,10},{7,11},{8,12},{9,13},{1... | collective-permute-start | bytes 10616840 | tf_op jit(solution)/shard_map/ppermute | solution.py:324
  266.7 178.5 %collective-permute-start.11 = (bf16[1536,1152]{1,0:T(8,128)(2,1)S(1)}, bf16[1536,1152]{1,0:T(8,128)(2,1)}, u32[]{:S(2)}, u32[]{:S(2)}) collective-permute-start(bf16[1536,1152]{1,0:T(8,128)(2,1)S(1)} %pad_maximum_fusion.1), channel_id=1, source_target_pairs={{0,3},{1,0},{2,1},{3,2},{4,7},{5,4},{6,5},{7,6},{8,11},{9,8},{10,9... | collective-permute-start | bytes 10616840 | tf_op jit(solution)/shard_map/ppermute | solution.py:324
  275.1 2.1 copy-start.10
  275.1 2.0 copy-start.11
  275.1 2.0 copy-start.12
  277.1 168.0 %collective-permute-start.9 = (bf16[1536,1152]{1,0:T(8,128)(2,1)}, bf16[1536,1152]{1,0:T(8,128)(2,1)}, u32[]{:S(2)}, u32[]{:S(2)}) collective-permute-start(bf16[1536,1152]{1,0:T(8,128)(2,1)} %pad_maximum_fusion), channel_id=1, source_target_pairs={{0,1},{1,2},{2,3},{3,0},{4,5},{5,6},{6,7},{7,4},{8,9},{9,10},{10,1... | collective-permute-start | bytes 10616840 | tf_op jit(solution)/shard_map/ppermute | solution.py:324
Sparse Core Ops, SparseCore 0:
  27.3 82.4 all-reduce.3
